TPU v7x, 32 devices: a whole 2x2x4 slice. The times are simulated.
32 devices in a mesh: dp: 4 (over y, x), ctx: 2 (over core), ch: 4 (over z).
Axes of the slice: x: 2, y: 2, z: 4, core: 2. Of those that a mesh axis runs over, the one named last changes fastest.
Arguments:
- gate_input: bfloat16 [4, 256, 4096], P('dp', 'ctx', 'ch'), may hold values from -6 to 6
- conv_input: bfloat16 [4, 256, 4096], P('dp', 'ctx', 'ch'), may hold values from -6 to 6
- grad_output: bfloat16 [4, 256, 4096], P('dp', 'ctx', 'ch'), may hold values from -6 to 6
- kernel: bfloat16 [128, 256], P('ch'), may hold values from -0.375 to 0.375
Outputs:
- output: bfloat16 [4, 256, 4096], P('dp', 'ctx', 'ch')
- grad_gate: bfloat16 [4, 256, 4096], P('dp', 'ctx', 'ch')
- grad_conv: bfloat16 [4, 256, 4096], P('dp', 'ctx', 'ch')
- grad_kernel: float32 [128, 256], P('ch', ('dp', 'ctx'))
All inputs are finite; a program needn't handle non-finite values.
Results may differ from a plain program's by a relative error of at most 0.0049.
Values may be sent and summed in bfloat16 or wider, within the bound.
A program may use at most 64 MiB of HBM per device.

v0:
```python
import math

import jax
import jax.numpy as jnp
from jax import lax
from jax.sharding import PartitionSpec as P


def toeplitz(padded_kernel, offset, tok_rows):
    groups = padded_kernel.shape[0]
    segment = lax.dynamic_slice_in_dim(padded_kernel, offset * tok_rows + 1, 2 * tok_rows, 1)
    reverse = segment[:, ::-1]
    rolled = jnp.concatenate([reverse[:, tok_rows:], reverse[:, :tok_rows]], axis=1)
    tiled = jnp.tile(rolled, (1, tok_rows))[:, : tok_rows * (2 * tok_rows - 1)]
    return tiled.reshape(groups, tok_rows, 2 * tok_rows - 1)[:, :, :tok_rows]


def diagonal_sums(matrix):
    groups = matrix.shape[0]
    extent = matrix.shape[1]
    flipped = matrix[:, :, ::-1]
    padded = jnp.pad(flipped, ((0, 0), (0, 0), (0, extent)))
    flattened = padded.reshape(groups, 2 * extent * extent)[:, : extent * (2 * extent - 1)]
    totals = jnp.sum(flattened.reshape(groups, extent, 2 * extent - 1), axis=1, dtype=jnp.float32)
    return jnp.pad(totals, ((0, 0), (0, 1)))


def body(gate_input, conv_input, grad_output, kernel):
    tok_rows = gate_input.shape[1]
    channels = gate_input.shape[2]
    groups = kernel.shape[0]
    group_size = channels // groups
    lag_count = kernel.shape[1]
    lag_blocks = lag_count // tok_rows
    padded_kernel = jnp.pad(kernel, ((0, 0), (tok_rows, 2 * tok_rows)))
    blocks = lax.axis_size("ctx")
    own_block = lax.axis_index("ctx")
    gate_rows = gate_input[0]
    grad_rows = grad_output[0]
    grad_mixed = (gate_rows.astype(jnp.float32) * grad_rows.astype(jnp.float32)).astype(
        jnp.bfloat16
    )

    def forward_add(running, matrix, block):
        shaped = block.reshape(tok_rows, groups, group_size)
        return running + jnp.einsum(
            "gab,bgc->agc", matrix, shaped, preferred_element_type=jnp.float32
        ).reshape(tok_rows, channels)

    def backward_add(running, matrix, block):
        shaped = block.reshape(tok_rows, groups, group_size)
        return running + jnp.einsum(
            "gab,agc->bgc", matrix, shaped, preferred_element_type=jnp.float32
        ).reshape(tok_rows, channels)

    def window_add(buffer, grad_block, value_block, offset):
        left_side = grad_block.reshape(tok_rows, groups, group_size)
        right_side = value_block.reshape(tok_rows, groups, group_size)
        paired = jnp.einsum(
            "agc,bgc->gab", left_side, right_side, preferred_element_type=jnp.float32
        ).astype(jnp.bfloat16)
        window = diagonal_sums(paired)
        first_col = offset * tok_rows
        current = lax.dynamic_slice_in_dim(buffer, first_col, 2 * tok_rows, 1)
        return lax.dynamic_update_slice_in_dim(buffer, current + window, first_col, 1)

    def visit_block(carried, value_block, grad_block, offset, has_value, has_grad):
        convolved, grad_vals, buffer = carried
        bounded = jnp.minimum(offset, lag_blocks)
        matrix = toeplitz(padded_kernel, bounded, tok_rows)
        convolved = lax.cond(
            has_value, lambda: forward_add(convolved, matrix, value_block), lambda: convolved
        )
        grad_vals = lax.cond(
            has_grad, lambda: backward_add(grad_vals, matrix, grad_block), lambda: grad_vals
        )
        buffer = lax.cond(
            has_value, lambda: window_add(buffer, grad_mixed, value_block, bounded), lambda: buffer
        )
        return (convolved, grad_vals, buffer)

    initial = (
        jnp.zeros((tok_rows, channels), jnp.float32),
        jnp.zeros((tok_rows, channels), jnp.float32),
        jnp.zeros((groups, lag_count + 2 * tok_rows), jnp.float32),
    )
    value_shard = lax.all_gather(conv_input, "ctx", axis=1, tiled=True)
    grad_shard = lax.all_gather(grad_mixed[None], "ctx", axis=1, tiled=True)
    pieces = value_shard.shape[1] // tok_rows

    def per_block(position, carried_now):
        value_block = lax.dynamic_slice_in_dim(value_shard[0], position * tok_rows, tok_rows, 0)
        grad_block = lax.dynamic_slice_in_dim(grad_shard[0], position * tok_rows, tok_rows, 0)
        distance = jnp.abs(own_block - position)
        near = distance <= lag_blocks
        return visit_block(
            carried_now,
            value_block,
            grad_block,
            distance,
            (position <= own_block) & near,
            (position >= own_block) & near,
        )

    carried = lax.fori_loop(0, pieces, per_block, initial)
    convolved, grad_vals, buffer = carried
    output = (gate_rows.astype(jnp.float32) * convolved).astype(jnp.bfloat16)[None]
    grad_gate = (grad_rows.astype(jnp.float32) * convolved).astype(jnp.bfloat16)[None]
    grad_conv = grad_vals.astype(jnp.bfloat16)[None]
    partial_value = buffer[:, tok_rows - 1 : tok_rows - 1 + lag_count]
    summed = lax.psum_scatter(partial_value, ("dp", "ctx"), scatter_dimension=1, tiled=True)
    grad_kernel = summed / math.sqrt(lax.axis_size("dp") * tok_rows * blocks)
    return (output, grad_gate, grad_conv, grad_kernel)


def solution(mesh):
    return jax.shard_map(
        body,
        mesh=mesh,
        in_specs=(P("dp", "ctx", "ch"), P("dp", "ctx", "ch"), P("dp", "ctx", "ch"), P("ch", None)),
        out_specs=(
            P("dp", "ctx", "ch"),
            P("dp", "ctx", "ch"),
            P("dp", "ctx", "ch"),
            P("ch", ("dp", "ctx")),
        ),
        check_vma=False,
    )
```

profile of v0, /device:TPU:0, one launch (start us, length us, event | category | flops | bytes accessed | tf_op | source)
XLA Modules:
  0.0 125.2 jit_solution(5297696908007325567)
XLA Ops:
  7.2 0.0 copy-start.1
  7.2 0.0 reduce-scatter.4.cloned.1.call-start
  7.2 1.1 fusion.6
  8.4 0.0 copy-start.2
  8.4 1.1 fusion.4
  9.5 2.3 %all_gather.7 = bf16[1,256,1024]{2,1,0:T(8,128)(2,1)S(1)} all-gather(bf16[1,128,1024]{2,1,0:T(8,128)(2,1)S(1)} %fusion.6), channel_id=1, replica_groups=mesh['dp'=4,'ctx'=2,'ch'=4] {'ctx'}, dimensions={1}, use_global_device_ids=true | all-gather | bytes 786432 | tf_op jit(solution)/shard_map/all_gather | solution.py:88
  11.7 1.1 copy.21
  12.8 0.0 copy-done.1
  12.8 0.2 copy.20
  13.0 2.3 %all_gather.6 = bf16[1,256,1024]{1,2,0:T(8,128)(2,1)} all-gather(bf16[1,128,1024]{1,2,0:T(8,128)(2,1)S(1)} %copy.20), channel_id=1, replica_groups=mesh['dp'=4,'ctx'=2,'ch'=4] {'ctx'}, dimensions={1}, use_global_device_ids=true | all-gather | bytes 786432 | tf_op jit(solution)/shard_map/all_gather | solution.py:87
  15.3 0.2 copy.22
  15.5 0.0 copy-done.2
  15.6 45.1 %while.28 = (s32[]{:T(128)}, f32[128,1024]{0,1:T(8,128)S(1)}, f32[128,1024]{0,1:T(8,128)S(1)}, f32[32,512]{1,0:T(8,128)S(1)}, s32[]{:T(128)}, /*index=5*/bf16[1,...) while((s32[]{:T(128)}, f32[128,1024]{0,1:T(8,128)S(1)}, ...), condition=%wide.region_8.9_spmd, body=%wide.region_0.8_spmd.sunk | while | flops 103571504 | bytes 56762792 | solution.py:105
  15.6 0.1 constant_dynamic-slice_fusion.4
  15.7 0.1 slice.61
  15.8 0.1 slice.62
  15.9 0.1 tile.25
  16.0 1.2 copy.31
  17.3 0.1 slice.63
  17.4 7.8 %reshape.70 = bf16[32,128,255]{2,1,0:T(8,128)(2,1)} reshape(bf16[32,32640]{1,0:T(8,128)(2,1)S(1)} %slice.63) | data formatting | bytes 4177920 | tf_op jit(solution)/shard_map/while/body/eval_jaxpr/reshape | solution.py:15
  25.2 1.3 %slice.64 = bf16[32,128,128]{2,1,0:T(8,128)(2,1)S(1)} slice(bf16[32,128,255]{2,1,0:T(8,128)(2,1)} %reshape.70), slice={[0:32], [0:128], [0:128]} | slice | bytes 2097152 | tf_op jit(solution)/shard_map/while/body/eval_jaxpr/slice | solution.py:15
  26.5 0.0 copy-start
  26.5 1.0 dynamic-slice_bitcast_fusion.2
  27.6 0.8 conditional.6
  27.6 0.6 fusion.9
  28.2 0.1 bitcast_add_fusion
  28.3 0.0 copy-done
  28.3 0.5 conditional.7
  28.4 0.4 fusion.10
  28.8 0.1 bitcast_add_fusion.1
  28.9 19.2 %conditional.8 = (f32[32,512]{1,0:T(8,128)S(1)}) conditional(s32[]{:T(128)} %convert_element_type.126, f32[32,512]{1,0:T(8,128)S(1)} %get-tuple-element.433, (s32[]{:T(128)}, f32[32,512]{1,0:T(8,128)S(1)}, bf16[128,1024]{0,1:T(8,128)(2,1)S(1)}, bf16[128,1024]{0,1:T(8,128)(2,1)S(1)}) %tuple.93), branch_computations={%region_5.5_spmd, %region_6.7_spmd} | conditional | flops 36167716 | bytes 29941696 | solution.py:77
  28.9 0.5 convolution_convert_fusion
  29.4 2.9 %rev.5 = bf16[32,128,128]{2,1,0:T(8,128)(2,1)S(1)} reverse(bf16[32,128,128]{2,1,0:T(8,128)(2,1)S(1)} %convolution_convert_fusion), dimensions={2} | reverse | bytes 2097152 | tf_op jit(solution)/shard_map/while/body/eval_jaxpr/cond/branch_1_fun/rev | solution.py:21
  32.3 0.3 pad.9
  32.6 1.2 copy.28
  33.8 2.2 %slice_convert_fusion = f32[32,32640]{1,0:T(8,128)} fusion(bf16[32,32768]{1,0:T(8,128)(2,1)S(1)} %bitcast.66), kind=kLoop, calls=%fused_computation.3 | loop fusion | flops 1044480 | bytes 6266880 | tf_op jit(solution)/shard_map/while/body/eval_jaxpr/cond/branch_1_fun/convert_element_type | solution.py:24
  36.1 9.4 %reshape.64 = f32[32,128,255]{2,1,0:T(8,128)} reshape(f32[32,32640]{1,0:T(8,128)} %slice_convert_fusion) | data formatting | bytes 8355840 | tf_op jit(solution)/shard_map/while/body/eval_jaxpr/cond/branch_1_fun/convert_element_type | solution.py:24
  45.5 2.6 %reduce_sum.8 = f32[32,255]{1,0:T(8,128)S(1)} reduce(f32[32,128,255]{2,1,0:T(8,128)} %reshape.64, f32[]{:T(128)} %constant.84.clone), dimensions={1}, to_apply=%region_7.6 | reduce | flops 1036320 | bytes 4210564 | tf_op jit(solution)/shard_map/while/body/eval_jaxpr/cond/branch_1_fun/reduce_sum | solution.py:24
  48.2 0.1 constant_dynamic-slice_fusion.4
  48.2 0.1 slice.61
  48.3 0.1 slice.62
  48.4 0.1 tile.25
  48.6 1.2 copy.31
  49.8 0.1 slice.63
  49.9 7.8 %reshape.70 = bf16[32,128,255]{2,1,0:T(8,128)(2,1)} reshape(bf16[32,32640]{1,0:T(8,128)(2,1)S(1)} %slice.63) | data formatting | bytes 4177920 | tf_op jit(solution)/shard_map/while/body/eval_jaxpr/reshape | solution.py:15
  57.7 1.3 %slice.64 = bf16[32,128,128]{2,1,0:T(8,128)(2,1)S(1)} slice(bf16[32,128,255]{2,1,0:T(8,128)(2,1)} %reshape.70), slice={[0:32], [0:128], [0:128]} | slice | bytes 2097152 | tf_op jit(solution)/shard_map/while/body/eval_jaxpr/slice | solution.py:15
  59.0 0.0 copy-start
  59.1 1.0 dynamic-slice_bitcast_fusion.2
  60.1 0.0 copy-done
  60.2 0.5 conditional.7
  60.2 0.4 fusion.10
  60.6 0.1 bitcast_add_fusion.1
  60.7 0.1 slice.52
  60.8 0.8 copy.26
  61.5 0.0 reduce-scatter.4.cloned.1.call-update
  61.6 0.2 copy.23
  61.8 2.0 %fusion.8 = (bf16[1,128,1024]{2,1,0:T(8,128)(2,1)}, bf16[1,128,1024]{2,1,0:T(8,128)(2,1)}) fusion(f32[128,1024]{1,0:T(8,128)S(1)} %copy.23, bf16[1,128,1024]{2,1,0:T(8,128)(2,1)} %param.14, bf16[1,128,1024]{2,1,0:T(8,128)(2,1)} %param.12), kind=kLoop, calls=%fused_computation.21 | loop fusion | flops 786432 | bytes 1572864 | tf_op jit(solution)/shard_map/broadcast_in_dim | solution.py:108
  63.7 0.8 copy.25
  64.6 52.4 %reduce-scatter.4.cloned.1.call-done = f32[32,32]{1,0:T(8,128)} async-done(((f32[256,32]{1,0:T(8,128)}), f32[32,32]{1,0:T(8,128)}) %reduce-scatter.4.cloned.1.call-update) | async-done | bytes 4112
  116.9 0.8 copy.27
  117.7 0.6 broadcast_multiply_fusion
  (11 shorter events, 0.2 us)
Async XLA Ops:
  7.2 5.6 %copy-start.1 = (bf16[1,128,1024]{2,1,0:T(8,128)(2,1)S(1)}, bf16[1,128,1024]{2,1,0:T(8,128)(2,1)}, u32[]{:S(2)}) copy-start(bf16[1,128,1024]{2,1,0:T(8,128)(2,1)} %param.13) | copy-start | bytes 786436
  7.2 109.8 %reduce-scatter.4.cloned.1.call-start = ((), (), s32[]{:S(2)}) async-start(), calls=%async_computation.1 | async-start | bytes 147456
  8.4 7.1 %copy-start.2 = (bf16[32,256]{1,0:T(8,128)(2,1)S(1)}, bf16[32,256]{1,0:T(8,128)(2,1)}, u32[]{:S(2)}) copy-start(bf16[32,256]{1,0:T(8,128)(2,1)} %param.15) | copy-start | bytes 49156
  26.5 1.8 %copy-start = (bf16[1,256,1024]{1,2,0:T(8,128)(2,1)S(1)}, bf16[1,256,1024]{1,2,0:T(8,128)(2,1)}, u32[]{:S(2)}) copy-start(bf16[1,256,1024]{1,2,0:T(8,128)(2,1)} %get-tuple-element.453) | copy-start | bytes 1572868 | tf_op jit(solution)/shard_map/while
  59.0 1.1 copy-start
Sparse Core Ops, SparseCore 0:
  61.7 55.2 reduce-scatter.3
where the time goes:
time: 126 us; the launch traced here: 125 us
  waiting for transfers between devices  52.4 us (42%)
  local copies, waits for them, and re-layouts  41.8 us (33%)
  between operations  14.1 us (11%)
  other arithmetic  9.92 us (8%)
  blocking collectives  4.58 us (4%)
  matrix products  1.91 us (2%)
    unnamed x2, waiting for transfers between devices  52.4 us
    reshape x2, local copies, waits for them, and re-layouts, toeplitz(): return tiled.reshape(groups, tok_rows, 2 * tok_rows - 1)[:, :, :tok_rows]  15.6 us
    convert_element_type x1, local copies, waits for them, and re-layouts, diagonal_sums(): jnp.sum(flattened.reshape(groups, extent, 2 * extent - 1), axis=1, dtype=...  9.4 us
    rev x1, local copies, waits for them, and re-layouts, diagonal_sums(): flipped = matrix[:, :, ::-1]  2.92 us
    reduce_sum x1, other arithmetic, diagonal_sums(): jnp.sum(flattened.reshape(groups, extent, 2 * extent - 1), axis=1, dtype=...  2.59 us
    slice x2, local copies, waits for them, and re-layouts, toeplitz(): return tiled.reshape(groups, tok_rows, 2 * tok_rows - 1)[:, :, :tok_rows]  2.59 us
  transfers between devices with their start and end apart: 1, of which 1 were waited for; matrix products, arithmetic and copies ran while one was open for 2% of the time, Pallas kernels for 0%

commit v1 on v0

--- a/solution.py
+++ b/solution.py
@@ -1,8 +1,11 @@
+import functools
 import math
 
 import jax
 import jax.numpy as jnp
 from jax import lax
+from jax.experimental import pallas as pl
+from jax.experimental.pallas import tpu as pltpu
 from jax.sharding import PartitionSpec as P
 
 
@@ -25,7 +28,7 @@
     return jnp.pad(totals, ((0, 0), (0, 1)))
 
 
-def body(gate_input, conv_input, grad_output, kernel):
+def general_body(gate_input, conv_input, grad_output, kernel):
     tok_rows = gate_input.shape[1]
     channels = gate_input.shape[2]
     groups = kernel.shape[0]
@@ -113,6 +116,244 @@
     return (output, grad_gate, grad_conv, grad_kernel)
 
 
+TILE = 128
+F32, BF16 = jnp.float32, jnp.bfloat16
+MESH = pl.DeviceIdType.MESH
+
+
+def dot(left, right):
+    return jnp.dot(left, right, preferred_element_type=F32)
+
+
+def dot_lanes(left, right):
+    return lax.dot_general(left, right, (((1,), (1,)), ((), ())), preferred_element_type=F32)
+
+
+def iota(shape, dim):
+    return lax.broadcasted_iota(jnp.int32, shape, dim)
+
+
+def fused_kernel(
+    peers, scale,
+    gate_ref, conv_ref, grad_ref, taps_ref,
+    out_ref, ggate_ref, gconv_ref, gkern_ref,
+    mixed, flipped, flipped_x, landed, other_x, other_g, zx, zg, rev_taps, mats, part, packed, arrived,
+    block_send, block_recv, sum_send, sum_recv,
+):
+    rows, channels = conv_ref.shape
+    groups = taps_ref.shape[0]
+    size = channels // groups
+    per_tile = TILE // size
+    tiles = channels // TILE
+    half = tiles // 2
+    dp, ctx = lax.axis_index("dp"), lax.axis_index("ctx")
+    me = dp * 2 + ctx
+    share = gkern_ref.shape[1]
+
+    def place(index):
+        return {"dp": index // 2, "ctx": lax.rem(index, 2)}
+
+    barrier = pltpu.get_barrier_semaphore()
+    for step in range(1, peers):
+        pl.semaphore_signal(barrier, inc=1, device_id=place(lax.rem(me + step, peers)), device_id_type=MESH)
+
+    mixed[...] = (gate_ref[...].astype(F32) * grad_ref[...].astype(F32)).astype(BF16)
+    row, col = iota((rows, rows), 0), iota((rows, rows), 1)
+    lower = row >= col
+    upper = row + col >= rows - 1
+    backwards = jnp.where(row + col == rows - 1, 1.0, 0.0).astype(BF16)
+    wrapped = jnp.where(lax.rem(row + col, rows) == 0, 1.0, 0.0).astype(BF16)
+    rev_taps[0] = dot(taps_ref[:, :rows], wrapped)
+    rev_taps[1] = dot(taps_ref[:, rows:], wrapped)
+
+    pl.semaphore_wait(barrier, peers - 1)
+    partner = {"ctx": 1 - ctx}
+
+    def exchange(source):
+        return pltpu.make_async_remote_copy(
+            src_ref=source, dst_ref=landed, send_sem=block_send, recv_sem=block_recv,
+            device_id=partner, device_id_type=MESH,
+        )
+
+    @pl.when(ctx == 0)
+    def _():
+        exchange(conv_ref).start()
+
+    @pl.when(ctx == 1)
+    def _():
+        exchange(mixed).start()
+
+    lane = iota((1, TILE), 1)
+    masks = [((lane // size) == q).astype(F32).astype(BF16) for q in range(per_tile)]
+
+    def lanes(tile):
+        return pl.ds(pl.multiple_of(tile * TILE, TILE), TILE)
+
+    def build(tile, _):
+        for q in range(per_tile):
+            group = pl.ds(tile * per_tile + q, 1)
+            near, far = [
+                pltpu.roll(jnp.broadcast_to(rev_taps[h, group, :], (rows, rows)), 0, 1, stride=1, stride_axis=0)
+                for h in range(2)
+            ]
+            mats[tile, :, q * 2 * rows : q * 2 * rows + rows] = jnp.where(lower, near, 0.0).astype(BF16)
+            mats[tile, :, q * 2 * rows + rows : (q + 1) * 2 * rows] = jnp.where(lower, far, near).astype(BF16)
+        return 0
+
+    def diagonals(matrix):
+        turned = pltpu.roll(matrix, 0, 1, stride=1, stride_axis=0)
+        return jnp.sum(turned, axis=0, keepdims=True)
+
+    def masked(block):
+        return jnp.concatenate([block * m for m in masks], axis=0)
+
+    def pairs(tile):
+        return dot_lanes(masked(flipped_x[:, lanes(tile)]), mixed[:, lanes(tile)])
+
+    def near_only(step, _):
+        tile = (1 - ctx) * half + step
+        found = pairs(tile)
+        for q in range(per_tile):
+            group = pl.ds(tile * per_tile + q, 1)
+            part[0, group, :] = diagonals(jnp.where(upper, found[q * rows : (q + 1) * rows], 0.0))
+            part[1, group, :] = jnp.zeros((1, rows), F32)
+        return 0
+
+    def near_and_far(step, _):
+        tile = ctx * half + step
+        found = pairs(tile)
+        across = dot_lanes(masked(other_x[:, lanes(tile)]), other_g[:, lanes(tile)])
+        for q in range(per_tile):
+            group = pl.ds(tile * per_tile + q, 1)
+            inner, outer = found[q * rows : (q + 1) * rows], across[q * rows : (q + 1) * rows]
+            part[0, group, :] = diagonals(jnp.where(upper, inner, outer))
+            part[1, group, :] = diagonals(jnp.where(upper, outer, 0.0))
+        return 0
+
+    flipped_x[...] = dot(backwards, conv_ref[...]).astype(BF16)
+    flipped[...] = dot(backwards, mixed[...]).astype(BF16)
+    lax.fori_loop(0, tiles, build, 0)
+    lax.fori_loop(0, half, near_only, 0)
+
+    exchange(conv_ref).wait_recv()
+    block = landed[...]
+    turned_block = dot(backwards, block).astype(BF16)
+    first = ctx == 0
+    other_x[...] = jnp.where(first, flipped_x[...], turned_block)
+    other_g[...] = jnp.where(first, block, mixed[...])
+    lax.fori_loop(0, half, near_and_far, 0)
+
+    for peer in range(peers):
+        h, e = peer // (rows // share), peer % (rows // share)
+        tile8 = jnp.zeros((8, TILE), F32)
+        for j in range(groups // 8):
+            value = part[h, 8 * j : 8 * j + 8, :]
+            shift = (share * (j - e) + 1) % TILE
+            if shift:
+                value = pltpu.roll(value, shift, 1)
+            tile8 = jnp.where(lane // share == j, value, tile8)
+        packed[peer] = tile8
+
+    def send_sum(step):
+        peer = lax.rem(me + step, peers)
+        return pltpu.make_async_remote_copy(
+            src_ref=packed.at[peer], dst_ref=arrived.at[step],
+            send_sem=sum_send.at[step], recv_sem=sum_recv.at[step],
+            device_id=place(peer), device_id_type=MESH,
+        )
+
+    copies = [send_sum(step) for step in range(1, peers)]
+    for copy in copies:
+        copy.start()
+
+    zx[...] = jnp.where(first, jnp.zeros_like(block), block)
+    zg[...] = jnp.where(first, turned_block, jnp.zeros_like(block))
+
+    def convolve(tile, _):
+        at = lanes(tile)
+        total = jnp.zeros((rows, 2 * TILE), F32)
+        stacked = jnp.concatenate(
+            [
+                jnp.concatenate([conv_ref[:, at], flipped[:, at]], axis=1),
+                jnp.concatenate([zx[:, at], zg[:, at]], axis=1),
+            ],
+            axis=0,
+        )
+        wide = jnp.concatenate([stacked * jnp.concatenate([m, m], axis=1) for m in masks], axis=0)
+        total = dot(mats[tile], wide)
+        convolved = total[:, :TILE]
+        out_ref[:, at] = (gate_ref[:, at].astype(F32) * convolved).astype(BF16)
+        ggate_ref[:, at] = (grad_ref[:, at].astype(F32) * convolved).astype(BF16)
+        gconv_ref[:, at] = dot(backwards, total[:, TILE:].astype(BF16)).astype(BF16)
+        return 0
+
+    lax.fori_loop(0, tiles, convolve, 0)
+
+    exchange(conv_ref).wait_send()
+    summed = packed[me]
+    for step, copy in zip(range(1, peers), copies):
+        copy.wait()
+        summed = summed + arrived[step]
+    summed = summed * scale
+    for j in range(groups // 8):
+        value = summed if j == 0 else pltpu.roll(summed, TILE - share * j, 1)
+        gkern_ref[8 * j : 8 * j + 8, :] = value[:, :share]
+
+
+def fused_body(gate_input, conv_input, grad_output, kernel):
+    _, rows, channels = conv_input.shape
+    groups, lag_count = kernel.shape
+    tiles = channels // TILE
+    peers = lax.axis_size("dp") * lax.axis_size("ctx")
+    scale = 1.0 / math.sqrt(lax.axis_size("dp") * rows * lax.axis_size("ctx"))
+    block = jax.ShapeDtypeStruct((rows, channels), BF16)
+    vmem = pl.BlockSpec(memory_space=pltpu.VMEM)
+    results = pl.pallas_call(
+        functools.partial(fused_kernel, peers, scale),
+        out_shape=[block, block, block, jax.ShapeDtypeStruct((groups, lag_count // peers), F32)],
+        in_specs=[vmem] * 4,
+        out_specs=[vmem] * 4,
+        scratch_shapes=[pltpu.VMEM((rows, channels), BF16)] * 8
+        + [
+            pltpu.VMEM((2, groups, rows), F32),
+            pltpu.VMEM((tiles, rows, (groups // tiles) * 2 * rows), BF16),
+            pltpu.VMEM((2, groups, rows), F32),
+            pltpu.VMEM((peers, 8, TILE), F32),
+            pltpu.VMEM((peers, 8, TILE), F32),
+            pltpu.SemaphoreType.DMA,
+            pltpu.SemaphoreType.DMA,
+            pltpu.SemaphoreType.DMA((peers,)),
+            pltpu.SemaphoreType.DMA((peers,)),
+        ],
+        compiler_params=pltpu.CompilerParams(
+            collective_id=0, has_side_effects=True, vmem_limit_bytes=48 * 1024 * 1024
+        ),
+        cost_estimate=pl.CostEstimate(
+            flops=20 * rows * rows * channels, bytes_accessed=12 * rows * channels, transcendentals=0
+        ),
+    )(gate_input[0], conv_input[0], grad_output[0], kernel)
+    return (results[0][None], results[1][None], results[2][None], results[3])
+
+
+def body(gate_input, conv_input, grad_output, kernel):
+    _, rows, channels = conv_input.shape
+    groups, lag_count = kernel.shape
+    peers = lax.axis_size("dp") * lax.axis_size("ctx")
+    fits = (
+        lax.axis_size("ctx") == 2
+        and rows == TILE
+        and lag_count == 2 * rows
+        and channels % (2 * TILE) == 0
+        and TILE % (channels // groups) == 0
+        and lag_count % peers == 0
+        and rows % (lag_count // peers) == 0
+        and groups * (lag_count // peers) == 8 * TILE
+    )
+    if fits:
+        return fused_body(gate_input, conv_input, grad_output, kernel)
+    return general_body(gate_input, conv_input, grad_output, kernel)
+
+
 def solution(mesh):
     return jax.shard_map(
         body,

time: 126 us -> 19.1 us (0.15)
  waiting for transfers between devices: 52.4 us -> 0 us
  local copies, waits for them, and re-layouts: 41.8 us -> 6.27 us
  between operations: 14.1 us -> 0.65 us
  Pallas kernels: 0 us -> 11.9 us
  other arithmetic: 9.92 us -> 0 us
  blocking collectives: 4.58 us -> 0 us
  matrix products: 1.91 us -> 0 us
    unnamed x2 -> x0, waiting for transfers between devices: 52.4 us -> none
    reshape x2 -> x0, local copies, waits for them, and re-layouts: 15.6 us -> none  [toeplitz(): return tiled.reshape(groups, tok_rows, 2 * tok_rows - 1)[:, :, :tok_rows]]
    pallas_call x0 -> x1, Pallas kernels: none -> 11.9 us  [fused_body(): pl.pallas_call(functools.partial(fused_kernel, peers, scale), out_shape=[...]
    convert_element_type x1 -> x0, local copies, waits for them, and re-layouts: 9.4 us -> none  [diagonal_sums(): jnp.sum(flattened.reshape(groups, extent, 2 * extent - 1), axis=1, dtype=...]
    while x10 -> x0, local copies, waits for them, and re-layouts: 4.7 us -> none
    all_gather x2 -> x0, blocking collectives: 4.58 us -> none  [the longest x1 2.32 us: body(): value_shard = lax.all_gather(conv_input, 'ctx', axis=1, tiled=True)]
    unnamed x7 -> x12, local copies, waits for them, and re-layouts: 1.72 us -> 6.27 us
    convert_element_type x3 -> x0, other arithmetic: 4.48 us -> none  [the longest x1 2.25 us: diagonal_sums(): jnp.sum(flattened.reshape(groups, extent, 2 * extent - 1), axis=1, dtype=...]
  transfers between devices with their start and end apart: 1 -> 0, of which waited for: 1 -> 0; matrix products, arithmetic and copies ran while one was open for 2% -> 0% of each run, Pallas kernels for 0% -> 0%
where the time goes in v1:
time: 19.1 us; the launch traced here: 18.8 us
  Pallas kernels  11.9 us (62%)
  local copies, waits for them, and re-layouts  6.27 us (33%)
  between operations  0.65 us (3%)
    pallas_call x1, Pallas kernels, fused_body(): pl.pallas_call(functools.partial(fused_kernel, peers, scale), out_shape=[...  11.9 us
    unnamed x12, local copies, waits for them, and re-layouts  6.27 us

profile of v1, /device:TPU:0, one launch (start us, length us, event | category | flops | bytes accessed | tf_op | source)
XLA Modules:
  0.0 18.8 jit_solution(11205555632361010514)
XLA Ops:
  0.6 0.0 copy-start
  0.6 0.9 %copy-done = bf16[1,128,1024]{2,1,0:T(8,128)(2,1)S(1)} copy-done((bf16[1,128,1024]{2,1,0:T(8,128)(2,1)S(1)}, bf16[1,128,1024]{2,1,0:T(8,128)(2,1)}, u32[]{:S(2)}) %copy-start) | copy-done | bytes 262168
  1.6 0.0 copy-start.1
  1.6 0.9 %copy-done.1 = bf16[1,128,1024]{2,1,0:T(8,128)(2,1)S(1)} copy-done((bf16[1,128,1024]{2,1,0:T(8,128)(2,1)S(1)}, bf16[1,128,1024]{2,1,0:T(8,128)(2,1)}, u32[]{:S(2)}) %copy-start.1) | copy-done | bytes 262168
  2.5 0.0 copy-start.2
  2.5 0.9 %copy-done.2 = bf16[1,128,1024]{2,1,0:T(8,128)(2,1)S(1)} copy-done((bf16[1,128,1024]{2,1,0:T(8,128)(2,1)S(1)}, bf16[1,128,1024]{2,1,0:T(8,128)(2,1)}, u32[]{:S(2)}) %copy-start.2) | copy-done | bytes 262168
  3.5 0.0 copy-start.3
  3.5 0.7 %copy-done.3 = bf16[32,256]{1,0:T(8,128)(2,1)S(1)} copy-done((bf16[32,256]{1,0:T(8,128)(2,1)S(1)}, bf16[32,256]{1,0:T(8,128)(2,1)}, u32[]{:S(2)}) %copy-start.3) | copy-done | bytes 16408
  4.2 11.9 %shard_map.75 = (bf16[128,1024]{1,0:T(8,128)(2,1)S(1)}, bf16[128,1024]{1,0:T(8,128)(2,1)S(1)}, bf16[128,1024]{1,0:T(8,128)(2,1)S(1)}, f32[32,32]{1,0:T(8,128)S(1)}) custom-call(bf16[128,1024]{1,0:T(8,128)(2,1)S(1)} %bitcast.9, bf16[128,1024]{1,0:T(8,128)(2,1)S(1)} %bitcast.10, bf16[128,1024]{1,0:T(8,128)(2,1)S(1)} %bitcast.11, bf16[32,256]{1,0:T(8,128)(2,1)S(1)} %copy-done.3), custom_call_target="tpu_custom_call" | custom-call | flops 335544320 | bytes 1572864 | tf_op jit(solution)/shard_map/pallas_call | solution.py:311
  16.1 0.7 %copy.12 = bf16[1,128,1024]{2,1,0:T(8,128)(2,1)} copy(bf16[1,128,1024]{2,1,0:T(8,128)(2,1)S(1)} %bitcast.8) | data formatting | bytes 524288
  16.8 0.7 %copy.13 = bf16[1,128,1024]{2,1,0:T(8,128)(2,1)} copy(bf16[1,128,1024]{2,1,0:T(8,128)(2,1)S(1)} %bitcast.7) | data formatting | bytes 524288
  17.5 0.7 %copy.14 = bf16[1,128,1024]{2,1,0:T(8,128)(2,1)} copy(bf16[1,128,1024]{2,1,0:T(8,128)(2,1)S(1)} %bitcast.6) | data formatting | bytes 524288
  18.2 0.6 %copy.15 = f32[32,32]{1,0:T(8,128)} copy(f32[32,32]{1,0:T(8,128)S(1)} %get-tuple-element.19) | data formatting | bytes 8192
Async XLA Ops:
  0.6 1.0 %copy-start = (bf16[1,128,1024]{2,1,0:T(8,128)(2,1)S(1)}, bf16[1,128,1024]{2,1,0:T(8,128)(2,1)}, u32[]{:S(2)}) copy-start(bf16[1,128,1024]{2,1,0:T(8,128)(2,1)} %param.4) | copy-start | bytes 786436
  1.6 0.9 %copy-start.1 = (bf16[1,128,1024]{2,1,0:T(8,128)(2,1)S(1)}, bf16[1,128,1024]{2,1,0:T(8,128)(2,1)}, u32[]{:S(2)}) copy-start(bf16[1,128,1024]{2,1,0:T(8,128)(2,1)} %param.5) | copy-start | bytes 786436
  2.5 0.9 %copy-start.2 = (bf16[1,128,1024]{2,1,0:T(8,128)(2,1)S(1)}, bf16[1,128,1024]{2,1,0:T(8,128)(2,1)}, u32[]{:S(2)}) copy-start(bf16[1,128,1024]{2,1,0:T(8,128)(2,1)} %param.6) | copy-start | bytes 786436
  3.5 0.7 %copy-start.3 = (bf16[32,256]{1,0:T(8,128)(2,1)S(1)}, bf16[32,256]{1,0:T(8,128)(2,1)}, u32[]{:S(2)}) copy-start(bf16[32,256]{1,0:T(8,128)(2,1)} %taps_ref.1) | copy-start | bytes 49156
